TPU v7x, 256 devices: a whole 4x4x8 slice. The times are simulated.
256 devices in a mesh: ctx: 32 (over z, x_lo, core), head: 8 (over x_hi, y).
Axes of the slice: x: 4 (x_hi: 2, x_lo: 2; x = x_hi * 2 + x_lo), y: 4, z: 8, core: 2. Of those that a mesh axis runs over, the one named last changes fastest.
Arguments:
- kv_latent: bfloat16 [16384, 576], P('ctx'), may hold values from -4 to 4
- queries: bfloat16 [16384, 3072], P('ctx', 'head'), may hold values from -22 to 22
- grad_out: bfloat16 [16384, 2048], P('ctx', 'head'), may hold values from -6 to 6
- kv_up_weight: bfloat16 [512, 4096], P(None, 'head'), may hold values from -0.25 to 0.25
- doc_ids: int32 [16384], replicated, may hold values from 0 to 15, never falling along the last dimension, each value on 1 to 1536 neighbouring positions
Outputs:
- grad_queries: bfloat16 [16384, 3072], P('ctx', 'head')
- grad_latent: bfloat16 [16384, 576], P('ctx')
- grad_weight: float32 [512, 4096], P('ctx', 'head')
Inputs may be any that keep to these rules, and one draw needn't show every extreme that they name: `doc_ids`: document ids never fall along the sequence; every document has 1 to 1536 tokens, and one has exactly 1536.
All inputs are finite; a program needn't handle non-finite values.
Results may differ from a plain program's by a relative error of at most 0.0076.
Values may be sent and summed in bfloat16 or wider, within the bound.
A program may use at most 64 MiB of HBM per device.

v0:
```python
import math
import jax
import jax.numpy as jnp
from jax import lax
from jax.sharding import PartitionSpec as P

NOPE = 128
ROPE = 64
VDIM = 128
LATENT = 512
REACH = 3
KEY_BLOCK = 512
masked_score = -1e30


def from_behind(value, axis, steps):
    count = lax.axis_size(axis)
    initial, last = (max(0, -steps), min(count, count - steps))
    return lax.ppermute(value, axis, [(source, source + steps) for source in range(initial, last)])


def local(kv_latent, queries, grad_out, kv_up_weight, doc_ids):
    row_count = kv_latent.shape[0]
    token_total = doc_ids.shape[0]
    head_count = kv_up_weight.shape[1] // (NOPE + VDIM)
    kv_width = head_count * (NOPE + VDIM)
    score_scale = 1.0 / math.sqrt(NOPE + ROPE)
    first_row = lax.axis_index("ctx") * row_count
    window_rows = (REACH + 1) * row_count
    window_start = first_row - REACH * row_count
    earlier = [kv_latent] + [
        from_behind(kv_latent, "ctx", offset) for offset in range(1, REACH + 1)
    ]
    stacked = jnp.concatenate(earlier[::-1], axis=0)
    lifted = jnp.dot(stacked[:, :LATENT], kv_up_weight, preferred_element_type=jnp.float32)
    key_side = jnp.concatenate([lifted.astype(jnp.bfloat16), stacked[:, LATENT:]], axis=1)
    query_heads = queries.reshape(row_count, head_count, NOPE + ROPE)
    query_nope = query_heads[:, :, :NOPE]
    query_rope = query_heads[:, :, NOPE:]
    out_heads = grad_out.reshape(row_count, head_count, VDIM)
    my_docs = lax.dynamic_slice_in_dim(doc_ids, first_row, row_count)
    query_pos = first_row + jnp.arange(row_count, dtype=jnp.int32)

    def block_parts(block_index):
        block_start = (block_index * KEY_BLOCK).astype(jnp.int32)
        key_rows = lax.dynamic_slice_in_dim(key_side, block_start, KEY_BLOCK, 0)
        pairs = key_rows[:, :kv_width].reshape(KEY_BLOCK, head_count, NOPE + VDIM)
        key_nope = pairs[:, :, :NOPE]
        values = pairs[:, :, NOPE:]
        key_rope = key_rows[:, kv_width:]
        key_pos = window_start + block_start + jnp.arange(KEY_BLOCK, dtype=jnp.int32)
        key_docs = jnp.take(doc_ids, jnp.clip(key_pos, 0, token_total - 1))
        visible = (
            (my_docs[:, None] == key_docs[None, :])
            & (key_pos[None, :] <= query_pos[:, None])
            & (key_pos[None, :] >= 0)
        )
        scores = score_scale * (
            jnp.einsum("thd,khd->htk", query_nope, key_nope, preferred_element_type=jnp.float32)
            + jnp.einsum("thd,kd->htk", query_rope, key_rope, preferred_element_type=jnp.float32)
        )
        scores = jnp.where(visible[None], scores, masked_score)
        grad_probs = jnp.einsum(
            "thd,khd->htk", out_heads, values, preferred_element_type=jnp.float32
        )
        return (key_nope, values, key_rope, visible, scores, grad_probs)

    block_total = window_rows // KEY_BLOCK
    block_first = 0

    def first_pass(block_index, carry):
        row_top, row_mass, row_cross = carry
        parts = block_parts(block_index)
        visible, scores, grad_probs = (parts[3], parts[4], parts[5])
        new_top = jnp.maximum(row_top, jnp.max(scores, axis=2))
        factor = jnp.exp(row_top - new_top)
        weights = jnp.where(visible[None], jnp.exp(scores - new_top[:, :, None]), 0.0)
        return (
            new_top,
            row_mass * factor + jnp.sum(weights, axis=2),
            row_cross * factor + jnp.sum(weights * grad_probs, axis=2),
        )

    stat_shape = (head_count, row_count)
    row_top, row_mass, row_cross = lax.fori_loop(
        block_first,
        block_total,
        first_pass,
        (
            jnp.full(stat_shape, masked_score, jnp.float32),
            jnp.zeros(stat_shape, jnp.float32),
            jnp.zeros(stat_shape, jnp.float32),
        ),
    )
    log_total = row_top + jnp.log(row_mass)
    delta = row_cross / row_mass

    def second_pass(block_index, carry):
        grad_qnope, grad_qrope, key_grads = carry
        key_nope, values, key_rope, visible, scores, grad_probs = block_parts(block_index)
        weights = jnp.where(visible[None], jnp.exp(scores - log_total[:, :, None]), 0.0)
        grad_scores = (weights * (grad_probs - delta[:, :, None])).astype(jnp.bfloat16)
        weights_low = weights.astype(jnp.bfloat16)
        grad_qnope = grad_qnope + score_scale * jnp.einsum(
            "htk,khd->thd", grad_scores, key_nope, preferred_element_type=jnp.float32
        )
        grad_qrope = grad_qrope + score_scale * jnp.einsum(
            "htk,kd->thd", grad_scores, key_rope, preferred_element_type=jnp.float32
        )
        grad_keys = score_scale * jnp.einsum(
            "htk,thd->khd", grad_scores, query_nope, preferred_element_type=jnp.float32
        )
        grad_rope = score_scale * jnp.einsum(
            "htk,thd->kd", grad_scores, query_rope, preferred_element_type=jnp.float32
        )
        grad_values = jnp.einsum(
            "htk,thd->khd", weights_low, out_heads, preferred_element_type=jnp.float32
        )
        block_grad = jnp.concatenate(
            [
                jnp.concatenate([grad_keys, grad_values], axis=2).reshape(KEY_BLOCK, kv_width),
                grad_rope,
            ],
            axis=1,
        )
        key_grads = lax.dynamic_update_slice_in_dim(
            key_grads, block_grad, (block_index * KEY_BLOCK).astype(jnp.int32), 0
        )
        return (grad_qnope, grad_qrope, key_grads)

    grad_qnope, grad_qrope, key_grads = lax.fori_loop(
        block_first,
        block_total,
        second_pass,
        (
            jnp.zeros((row_count, head_count, NOPE), jnp.float32),
            jnp.zeros((row_count, head_count, ROPE), jnp.float32),
            jnp.zeros((window_rows, kv_width + ROPE), jnp.float32),
        ),
    )

    def owner_part(offset):
        return key_grads[(REACH - offset) * row_count : (REACH - offset + 1) * row_count]

    summed = owner_part(0)
    for offset in range(1, REACH + 1):
        summed = summed + from_behind(owner_part(offset), "ctx", -offset)
    kv_grad = summed[:, :kv_width].astype(jnp.bfloat16)
    rope_grad = summed[:, kv_width:]
    latent_part = lax.dot_general(
        kv_grad, kv_up_weight, (((1,), (1,)), ((), ())), preferred_element_type=jnp.float32
    )
    latent_total = lax.psum(jnp.concatenate([latent_part, rope_grad], axis=1), "head")
    latent_cols = lax.slice_in_dim(
        kv_latent, 0, lax.axis_size("ctx") * (LATENT // lax.axis_size("ctx")), axis=1
    )
    grad_weight = lax.psum_scatter(
        lax.dot_general(
            latent_cols, kv_grad, (((0,), (0,)), ((), ())), preferred_element_type=jnp.float32
        ),
        "ctx",
        scatter_dimension=0,
        tiled=True,
    )
    grad_queries = (
        jnp.concatenate([grad_qnope, grad_qrope], axis=2)
        .reshape(row_count, head_count * (NOPE + ROPE))
        .astype(jnp.bfloat16)
    )
    return (grad_queries, latent_total.astype(jnp.bfloat16), grad_weight)


def solution(mesh):
    return jax.shard_map(
        local,
        mesh=mesh,
        in_specs=(P("ctx", None), P("ctx", "head"), P("ctx", "head"), P(None, "head"), P()),
        out_specs=(P("ctx", "head"), P("ctx", None), P("ctx", "head")),
        check_vma=False,
    )
```

profile of v0, /device:TPU:24, one launch (start us, length us, event | category | flops | bytes accessed | tf_op | source)
XLA Modules:
  0.0 333.0 jit_solution(5811115365233028075)
XLA Ops:
  7.2 3.8 %collective-permute-start = (bf16[512,576]{0,1:T(8,128)(2,1)}, bf16[512,576]{0,1:T(8,128)(2,1)}, u32[]{:S(2)}, u32[]{:S(2)}) collective-permute-start(bf16[512,576]{0,1:T(8,128)(2,1)} %param.11), channel_id=1, source_target_pairs={{0,24},{8,32},{16,40},{24,48},{32,56},{40,64},{48,72},{56,80},{64,... | collective-permute-start | bytes 1769480 | tf_op jit(solution)/shard_map/ppermute | solution.py:19
  11.0 4.6 %collective-permute-start.1 = (bf16[512,576]{0,1:T(8,128)(2,1)}, bf16[512,576]{0,1:T(8,128)(2,1)}, u32[]{:S(2)}, u32[]{:S(2)}) collective-permute-start(bf16[512,576]{0,1:T(8,128)(2,1)} %param.11), channel_id=1, source_target_pairs={{0,16},{8,24},{16,32},{24,40},{32,48},{40,56},{48,64},{56,72},{64,... | collective-permute-start | bytes 1769480 | tf_op jit(solution)/shard_map/ppermute | solution.py:19
  15.6 1.6 collective-permute-start.2
  17.2 1.2 copy.52
  18.5 1.1 copy.53
  19.6 0.8 copy.55
  20.7 1.1 constant_dynamic-update-slice_fusion.3
  21.8 11.4 %collective-permute-done.1 = bf16[512,576]{0,1:T(8,128)(2,1)} collective-permute-done((bf16[512,576]{0,1:T(8,128)(2,1)}, bf16[512,576]{0,1:T(8,128)(2,1)}, u32[]{:S(2)}, u32[]{:S(2)}) %collective-permute-start.1) | collective-permute-done | bytes 589856 | tf_op jit(solution)/shard_map/ppermute | solution.py:19
  33.3 1.1 constant_dynamic-update-slice_fusion.2
  34.6 1.3 convolution_convert_fusion
  36.0 1.7 pad_maximum_fusion.1
  37.7 32.1 %while.36 = (s32[]{:T(128)}, f32[2,512]{1,0:T(2,128)S(1)}, f32[2,512]{1,0:T(2,128)S(1)}, f32[2,512]{1,0:T(2,128)S(1)}, s32[512]{0:T(512)S(1)}, /*index=5*/s32[]{...) while((s32[]{:T(128)}, f32[2,512]{1,0:T(2,128)S(1)}, ...), condition=%wide.region_4.6_spmd.clone, body=%wide.region_0.5_spmd.clone.sunk | while | flops 342376960 | bytes 13933842 | solution.py:85
  37.8 3.1 gather_fusion
  41.2 1.1 constant_dynamic-slice_fusion.4
  42.8 1.6 fusion.95
  44.4 0.8 fusion.97
  45.8 3.1 gather_fusion
  49.3 1.1 constant_dynamic-slice_fusion.4
  50.3 0.5 fusion.93
  50.8 1.6 fusion.95
  52.4 0.8 fusion.97
  53.8 3.1 gather_fusion
  57.3 1.1 constant_dynamic-slice_fusion.4
  58.9 1.6 fusion.95
  60.4 0.8 fusion.97
  61.8 3.1 gather_fusion
  65.3 1.1 constant_dynamic-slice_fusion.4
  66.9 1.6 fusion.95
  68.5 0.8 fusion.97
  69.8 2.7 broadcast_in_dim.131
  72.5 46.1 %while.37 = (s32[]{:T(128)}, f32[512,2,128]{0,2,1:T(8,128)S(1)}, f32[512,2,64]{0,2,1:T(8,128)S(1)}, f32[2048,576]{0,1:T(8,128)}, bf16[2048,576]{0,1:T(8,128)(2,1...) while((s32[]{:T(128)}, f32[512,2,128]{0,2,1:T(8,128)S(1)}, ...), condition=%wide.region_6.8_spmd.clone, body=%wide.region_5.7_spmd.clone.sunk | while | flops 879502848 | bytes 26778924 | solution.py:131
  72.6 3.1 gather_fusion.1
  76.0 1.1 constant_dynamic-slice_fusion.5
  77.6 1.8 fusion.116
  81.2 1.2 fusion.119
  82.9 1.2 maximum_dynamic-update-slice_fusion.2
  84.1 3.1 gather_fusion.1
  87.6 1.1 constant_dynamic-slice_fusion.5
  89.1 1.8 fusion.116
  92.7 1.2 fusion.119
  94.4 1.2 maximum_dynamic-update-slice_fusion.2
  95.7 3.1 gather_fusion.1
  99.2 1.1 constant_dynamic-slice_fusion.5
  100.7 1.7 fusion.116
  104.3 1.2 fusion.119
  106.0 1.1 maximum_dynamic-update-slice_fusion.2
  107.2 3.1 gather_fusion.1
  110.7 1.1 constant_dynamic-slice_fusion.5
  112.2 1.7 fusion.116
  115.8 1.2 fusion.119
  117.5 1.1 maximum_dynamic-update-slice_fusion.2
  118.6 2.3 fusion.37
  121.0 1.3 collective-permute-start.3
  122.3 1.3 collective-permute-start.5
  123.6 1.4 collective-permute-start.4
  125.0 2.8 collective-permute-done.3
  127.8 34.0 %collective-permute-done.5 = f32[512,576]{0,1:T(8,128)S(1)} collective-permute-done((f32[512,576]{0,1:T(8,128)S(1)}, f32[512,576]{0,1:T(8,128)S(1)}, u32[]{:S(2)}, u32[]{:S(2)}) %collective-permute-start.5) | collective-permute-done | bytes 1179680 | tf_op jit(solution)/shard_map/ppermute | solution.py:19
  161.8 12.1 %collective-permute-done.4 = f32[512,576]{0,1:T(8,128)S(1)} collective-permute-done((f32[512,576]{0,1:T(8,128)S(1)}, f32[512,576]{0,1:T(8,128)S(1)}, u32[]{:S(2)}, u32[]{:S(2)}) %collective-permute-start.4) | collective-permute-done | bytes 1179680 | tf_op jit(solution)/shard_map/ppermute | solution.py:19
  173.9 1.8 add_add_fusion
  175.7 1.4 convolution_bitcast_fusion.2
  177.2 2.6 copy.66
  179.9 0.9 copy.56
  181.4 93.4 %all-reduce.1 = bf16[512,576]{0,1:T(8,128)(2,1)} all-reduce(f32[512,576]{0,1:T(8,128)S(1)} %pad_maximum_fusion.2), channel_id=1, replica_groups=mesh['ctx'=32,'head'=8] {'head'}, use_global_device_ids=true, to_apply=%region_7.9 | all-reduce | flops 294912 | bytes 1769472 | tf_op jit(solution)/shard_map/psum | solution.py:153
  274.8 51.4 %reduce-scatter.4.cloned.1.call-done = f32[16,512]{1,0:T(8,128)} async-done(((f32[512,512]{1,0:T(8,128)}), f32[16,512]{1,0:T(8,128)}) %reduce-scatter.4.cloned.1.call-update) | async-done | bytes 32784
  (128 shorter events, 18.4 us)
Async XLA Ops:
  7.2 27.5 %copy-start = (bf16[512,512]{1,0:T(8,128)(2,1)S(1)}, bf16[512,512]{1,0:T(8,128)(2,1)}, u32[]{:S(2)}) copy-start(bf16[512,512]{1,0:T(8,128)(2,1)} %param.14) | copy-start | bytes 1572868
  7.2 13.4 %copy-start.1 = (s32[16384]{0:T(1024)S(1)}, s32[16384]{0:T(1024)}, u32[]{:S(2)}) copy-start(s32[16384]{0:T(1024)} %param.15) | copy-start | bytes 196612
  7.2 319.0 %reduce-scatter.4.cloned.1.call-start = ((), (), s32[]{:S(2)}) async-start(), calls=%async_computation.1 | async-start | bytes 1081344
  7.2 13.5 %collective-permute-start = (bf16[512,576]{0,1:T(8,128)(2,1)}, bf16[512,576]{0,1:T(8,128)(2,1)}, u32[]{:S(2)}, u32[]{:S(2)}) collective-permute-start(bf16[512,576]{0,1:T(8,128)(2,1)} %param.11), channel_id=1, source_target_pairs={{0,24},{8,32},{16,40},{24,48},{32,56},{40,64},{48,72},{56,80},{64,... | collective-permute-start | bytes 1769480 | tf_op jit(solution)/shard_map/ppermute | solution.py:19
  11.0 22.2 %collective-permute-start.1 = (bf16[512,576]{0,1:T(8,128)(2,1)}, bf16[512,576]{0,1:T(8,128)(2,1)}, u32[]{:S(2)}, u32[]{:S(2)}) collective-permute-start(bf16[512,576]{0,1:T(8,128)(2,1)} %param.11), channel_id=1, source_target_pairs={{0,16},{8,24},{16,32},{24,40},{32,48},{40,56},{48,64},{56,72},{64,... | collective-permute-start | bytes 1769480 | tf_op jit(solution)/shard_map/ppermute | solution.py:19
  15.6 18.8 %collective-permute-start.2 = (bf16[512,576]{0,1:T(8,128)(2,1)}, bf16[512,576]{0,1:T(8,128)(2,1)S(1)}, u32[]{:S(2)}, u32[]{:S(2)}) collective-permute-start(bf16[512,576]{0,1:T(8,128)(2,1)} %param.11), channel_id=1, source_target_pairs={{0,8},{8,16},{16,24},{24,32},{32,40},{40,48},{48,56},{56,64},{64,7... | collective-permute-start | bytes 1769480 | tf_op jit(solution)/shard_map/ppermute | solution.py:19
  20.4 14.1 %copy-start.2 = (bf16[512,576]{0,1:T(8,128)(2,1)S(1)}, bf16[512,576]{0,1:T(8,128)(2,1)}, u32[]{:S(2)}) copy-start(bf16[512,576]{0,1:T(8,128)(2,1)} %param.11) | copy-start | bytes 1769476
  36.0 1.7 copy-start.4
  121.0 6.8 %collective-permute-start.3 = (f32[512,576]{0,1:T(8,128)S(1)}, f32[512,576]{0,1:T(8,128)S(1)}, u32[]{:S(2)}, u32[]{:S(2)}) collective-permute-start(f32[512,576]{0,1:T(8,128)S(1)} %get-tuple-element.637), channel_id=1, source_target_pairs={{8,0},{16,8},{24,16},{32,24},{40,32},{48,40},{56,48},{64,56},{72,6... | collective-permute-start | bytes 3538952 | tf_op jit(solution)/shard_map/ppermute | solution.py:19
  122.3 39.5 %collective-permute-start.5 = (f32[512,576]{0,1:T(8,128)S(1)}, f32[512,576]{0,1:T(8,128)S(1)}, u32[]{:S(2)}, u32[]{:S(2)}) collective-permute-start(f32[512,576]{0,1:T(8,128)S(1)} %get-tuple-element.638), channel_id=1, source_target_pairs={{24,0},{32,8},{40,16},{48,24},{56,32},{64,40},{72,48},{80,56},{88,... | collective-permute-start | bytes 3538952 | tf_op jit(solution)/shard_map/ppermute | solution.py:19
  123.6 52.1 %copy-start.3 = (bf16[512,576]{0,1:T(8,128)(2,1)S(1)}, bf16[512,576]{0,1:T(8,128)(2,1)}, u32[]{:S(2)}) copy-start(bf16[512,576]{0,1:T(8,128)(2,1)} %param.11) | copy-start | bytes 1769476
  123.6 50.3 %collective-permute-start.4 = (f32[512,576]{0,1:T(8,128)S(1)}, f32[512,576]{0,1:T(8,128)S(1)}, u32[]{:S(2)}, u32[]{:S(2)}) collective-permute-start(f32[512,576]{0,1:T(8,128)S(1)} %get-tuple-element.639), channel_id=1, source_target_pairs={{16,0},{24,8},{32,16},{40,24},{48,32},{56,40},{64,48},{72,56},{80,... | collective-permute-start | bytes 3538952 | tf_op jit(solution)/shard_map/ppermute | solution.py:19
Sparse Core Ops, SparseCore 0:
  179.9 146.2 reduce-scatter.3
where the time goes:
time: 334 us; the launch traced here: 333 us
  waiting for transfers between devices  112 us (34%)
  blocking collectives  93.4 us (28%)
  local copies, waits for them, and re-layouts  48.3 us (14%)
  matrix products  37.2 us (11%)
  between operations  14.3 us (4%)
  starting transfers between devices  14 us (4%)
  other arithmetic  13.3 us (4%)
    psum x1, blocking collectives, local(): lax.psum(jnp.concatenate([latent_part, rope_grad], axis=1), 'head')  93.4 us
    ppermute x6, waiting for transfers between devices, from_behind(): lax.ppermute(value, axis, [(source, source + steps) for source in range(i...  60.3 us
    unnamed x2, waiting for transfers between devices  51.4 us
    gather x8, local copies, waits for them, and re-layouts, block_parts(): key_docs = jnp.take(doc_ids, jnp.clip(key_pos, 0, token_total - 1))  25.1 us
    ppermute x6, starting transfers between devices, from_behind(): lax.ppermute(value, axis, [(source, source + steps) for source in range(i...  14 us
    dot_general x8, matrix products, block_parts(): jnp.einsum('thd,kd->htk', query_rope, key_rope, preferred_element_type=jn...  13.2 us
    unnamed x19, local copies, waits for them, and re-layouts  9.15 us
    slice x8, local copies, waits for them, and re-layouts, block_parts(): pairs = key_rows[:, :kv_width].reshape(KEY_BLOCK, head_count, NOPE + VDIM)  8.67 us
  transfers between devices with their start and end apart: 7, of which 5 were waited for; matrix products, arithmetic and copies ran while one was open for 2% of the time, Pallas kernels for 0%

commit v1 on v0

--- a/solution.py
+++ b/solution.py
@@ -150,7 +150,9 @@
     latent_part = lax.dot_general(
         kv_grad, kv_up_weight, (((1,), (1,)), ((), ())), preferred_element_type=jnp.float32
     )
-    latent_total = lax.psum(jnp.concatenate([latent_part, rope_grad], axis=1), "head")
+    block = jnp.concatenate([latent_part, rope_grad], axis=1)
+    pieces = lax.all_gather(block, "head", axis=0, tiled=False)
+    latent_total = pieces.sum(axis=0)
     latent_cols = lax.slice_in_dim(
         kv_latent, 0, lax.axis_size("ctx") * (LATENT // lax.axis_size("ctx")), axis=1
     )

time: 334 us -> 385 us (1.15)
  waiting for transfers between devices: 112 us -> 237 us
  blocking collectives: 93.4 us -> 0 us
  local copies, waits for them, and re-layouts: 48.3 us -> 59.9 us
  other arithmetic: 13.3 us -> 18.9 us
    all_gather x0 -> x1, waiting for transfers between devices: none -> 145 us  [local(): pieces = lax.all_gather(block, 'head', axis=0, tiled=False)]
    psum x1 -> x0, blocking collectives: 93.4 us -> none  [local(): lax.psum(jnp.concatenate([latent_part, rope_grad], axis=1), 'head')]
    unnamed x2 -> x3, waiting for transfers between devices: 51.4 us -> 31 us
    unnamed x19 -> x18, local copies, waits for them, and re-layouts: 9.15 us -> 20.8 us
    reduce_sum x0 -> x1, other arithmetic: none -> 4.56 us  [local(): latent_total = pieces.sum(axis=0)]
  transfers between devices with their start and end apart: 7 -> 8, of which waited for: 5 -> 6; matrix products, arithmetic and copies ran while one was open for 2% -> 7% of each run, Pallas kernels for 0% -> 0%
where the time goes in v1:
time: 385 us; the launch traced here: 383 us
  waiting for transfers between devices  237 us (62%)
  local copies, waits for them, and re-layouts  59.9 us (16%)
  matrix products  37.2 us (10%)
  other arithmetic  18.9 us (5%)
  between operations  15.8 us (4%)
  starting transfers between devices  14.1 us (4%)
    all_gather x1, waiting for transfers between devices, local(): pieces = lax.all_gather(block, 'head', axis=0, tiled=False)  145 us
    ppermute x6, waiting for transfers between devices, from_behind(): lax.ppermute(value, axis, [(source, source + steps) for source in range(i...  60.4 us
    unnamed x3, waiting for transfers between devices  31 us
    gather x8, local copies, waits for them, and re-layouts, block_parts(): key_docs = jnp.take(doc_ids, jnp.clip(key_pos, 0, token_total - 1))  25.1 us
    unnamed x18, local copies, waits for them, and re-layouts  20.8 us
    ppermute x6, starting transfers between devices, from_behind(): lax.ppermute(value, axis, [(source, source + steps) for source in range(i...  13.8 us
    dot_general x8, matrix products, block_parts(): jnp.einsum('thd,kd->htk', query_rope, key_rope, preferred_element_type=jn...  13.2 us
    slice x8, local copies, waits for them, and re-layouts, block_parts(): pairs = key_rows[:, :kv_width].reshape(KEY_BLOCK, head_count, NOPE + VDIM)  8.67 us
  transfers between devices with their start and end apart: 8, of which 6 were waited for; matrix products, arithmetic and copies ran while one was open for 7% of the time, Pallas kernels for 0%

profile of v1, /device:TPU:24, one launch (start us, length us, event | category | flops | bytes accessed | tf_op | source)
XLA Modules:
  0.0 383.3 jit_solution(459882192040848725)
XLA Ops:
  8.1 3.8 collective-permute-start
  11.9 4.6 %collective-permute-start.1 = (bf16[512,576]{0,1:T(8,128)(2,1)}, bf16[512,576]{0,1:T(8,128)(2,1)}, u32[]{:S(2)}, u32[]{:S(2)}) collective-permute-start(bf16[512,576]{0,1:T(8,128)(2,1)} %param.11), channel_id=1, source_target_pairs={{0,16},{8,24},{16,32},{24,40},{32,48},{40,56},{48,64},{56,72},{64,... | collective-permute-start | bytes 1769480 | tf_op jit(solution)/shard_map/ppermute | solution.py:19
  16.5 1.6 collective-permute-start.2
  18.1 1.2 copy.52
  19.3 1.1 copy.53
  20.4 0.8 copy.55
  21.5 1.1 constant_dynamic-update-slice_fusion.3
  22.7 11.4 %collective-permute-done.1 = bf16[512,576]{0,1:T(8,128)(2,1)} collective-permute-done((bf16[512,576]{0,1:T(8,128)(2,1)}, bf16[512,576]{0,1:T(8,128)(2,1)}, u32[]{:S(2)}, u32[]{:S(2)}) %collective-permute-start.1) | collective-permute-done | bytes 589856 | tf_op jit(solution)/shard_map/ppermute | solution.py:19
  34.1 1.1 constant_dynamic-update-slice_fusion.2
  35.5 1.3 convolution_convert_fusion
  36.8 1.7 pad_maximum_fusion.1
  38.5 32.1 %while.36 = (s32[]{:T(128)}, f32[2,512]{1,0:T(2,128)S(1)}, f32[2,512]{1,0:T(2,128)S(1)}, f32[2,512]{1,0:T(2,128)S(1)}, s32[512]{0:T(512)S(1)}, /*index=5*/s32[]{...) while((s32[]{:T(128)}, f32[2,512]{1,0:T(2,128)S(1)}, ...), condition=%wide.region_4.6_spmd.clone, body=%wide.region_0.5_spmd.clone.sunk | while | flops 342376960 | bytes 13933842 | solution.py:85
  38.6 3.1 gather_fusion
  42.1 1.1 constant_dynamic-slice_fusion.4
  43.6 1.6 fusion.95
  45.2 0.8 fusion.97
  46.6 3.1 gather_fusion
  50.1 1.1 constant_dynamic-slice_fusion.4
  51.7 1.6 fusion.95
  53.2 0.8 fusion.97
  54.6 3.1 gather_fusion
  58.1 1.1 constant_dynamic-slice_fusion.4
  59.7 1.6 fusion.95
  62.6 3.1 gather_fusion
  66.1 1.1 constant_dynamic-slice_fusion.4
  67.7 1.6 fusion.95
  70.6 2.7 broadcast_in_dim.131
  73.3 46.1 %while.37 = (s32[]{:T(128)}, f32[512,2,128]{0,2,1:T(8,128)S(1)}, f32[512,2,64]{0,2,1:T(8,128)S(1)}, f32[2048,576]{0,1:T(8,128)}, bf16[2048,576]{0,1:T(8,128)(2,1...) while((s32[]{:T(128)}, f32[512,2,128]{0,2,1:T(8,128)S(1)}, ...), condition=%wide.region_6.8_spmd.clone, body=%wide.region_5.7_spmd.clone.sunk | while | flops 879502848 | bytes 26778924 | solution.py:131
  73.4 3.1 gather_fusion.1
  76.9 1.1 constant_dynamic-slice_fusion.5
  78.4 1.7 fusion.116
  82.0 1.2 fusion.119
  83.7 1.1 maximum_dynamic-update-slice_fusion.2
  84.9 3.1 gather_fusion.1
  88.4 1.1 constant_dynamic-slice_fusion.5
  89.9 1.7 fusion.116
  93.5 1.2 fusion.119
  95.2 1.1 maximum_dynamic-update-slice_fusion.2
  96.4 3.1 gather_fusion.1
  99.9 1.1 constant_dynamic-slice_fusion.5
  101.4 1.7 fusion.116
  105.0 1.2 fusion.119
  106.7 1.2 maximum_dynamic-update-slice_fusion.2
  107.9 3.1 gather_fusion.1
  111.4 1.1 constant_dynamic-slice_fusion.5
  113.0 1.7 fusion.116
  116.5 1.2 fusion.119
  118.2 1.2 maximum_dynamic-update-slice_fusion.2
  119.4 2.3 fusion.37
  121.8 1.3 collective-permute-start.3
  123.1 1.3 collective-permute-start.5
  124.4 1.3 collective-permute-start.4
  125.7 2.9 collective-permute-done.3
  128.6 34.0 %collective-permute-done.5 = f32[512,576]{0,1:T(8,128)S(1)} collective-permute-done((f32[512,576]{0,1:T(8,128)S(1)}, f32[512,576]{0,1:T(8,128)S(1)}, u32[]{:S(2)}, u32[]{:S(2)}) %collective-permute-start.5) | collective-permute-done | bytes 1179680 | tf_op jit(solution)/shard_map/ppermute | solution.py:19
  162.6 12.1 %collective-permute-done.4 = f32[512,576]{0,1:T(8,128)S(1)} collective-permute-done((f32[512,576]{0,1:T(8,128)S(1)}, f32[512,576]{0,1:T(8,128)S(1)}, u32[]{:S(2)}, u32[]{:S(2)}) %collective-permute-start.4) | collective-permute-done | bytes 1179680 | tf_op jit(solution)/shard_map/ppermute | solution.py:19
  174.7 1.8 add_add_fusion
  177.0 1.1 pad_maximum_fusion.2
  178.3 1.5 convolution_bitcast_fusion.2
  179.8 1.3 copy.66
  181.3 0.9 copy.56
  182.2 145.3 %all-gather.3.cloned.1.call-done = f32[4096,576]{0,1:T(8,128)} async-done(((f32[512,576]{0,1:T(8,128)}), f32[4096,576]{0,1:T(8,128)}) %all-gather.3.cloned.1.call-update) | async-done | bytes 9437200 | tf_op jit(solution)/shard_map/all_gather | solution.py:154
  327.5 12.9 %copy.72 = f32[72,8,8,512]{3,2,1,0:T(8,128)S(1)} copy(f32[72,8,8,512]{3,1,2,0:T(8,128)} %bitcast.148) | data formatting | bytes 18874368
  340.4 4.6 %bitcast_reduce_fusion = bf16[512,576]{0,1:T(8,128)(2,1)} fusion(f32[72,8,8,512]{3,2,1,0:T(8,128)S(1)} %copy.72), kind=kLoop, calls=%fused_computation.65 | loop fusion | flops 2064384 | bytes 10027008 | tf_op jit(solution)/shard_map/reduce_sum | solution.py:155
  344.9 30.9 %reduce-scatter.4.cloned.1.call-done = f32[16,512]{1,0:T(8,128)} async-done(((f32[512,512]{1,0:T(8,128)}), f32[16,512]{1,0:T(8,128)}) %reduce-scatter.4.cloned.1.call-update) | async-done | bytes 32784
  (130 shorter events, 20.7 us)
Async XLA Ops:
  8.0 27.5 %copy-start = (bf16[512,512]{1,0:T(8,128)(2,1)S(1)}, bf16[512,512]{1,0:T(8,128)(2,1)}, u32[]{:S(2)}) copy-start(bf16[512,512]{1,0:T(8,128)(2,1)} %param.14) | copy-start | bytes 1572868
  8.0 13.4 %copy-start.1 = (s32[16384]{0:T(1024)S(1)}, s32[16384]{0:T(1024)}, u32[]{:S(2)}) copy-start(s32[16384]{0:T(1024)} %param.15) | copy-start | bytes 196612
  8.0 319.5 %all-gather.3.cloned.1.call-start = ((), (), s32[]{:S(2)}) async-start(), calls=%async_computation.1 | async-start | bytes 10616832 | tf_op jit(solution)/shard_map/all_gather | solution.py:154
  8.1 13.5 %collective-permute-start = (bf16[512,576]{0,1:T(8,128)(2,1)}, bf16[512,576]{0,1:T(8,128)(2,1)}, u32[]{:S(2)}, u32[]{:S(2)}) collective-permute-start(bf16[512,576]{0,1:T(8,128)(2,1)} %param.11), channel_id=1, source_target_pairs={{0,24},{8,32},{16,40},{24,48},{32,56},{40,64},{48,72},{56,80},{64,... | collective-permute-start | bytes 1769480 | tf_op jit(solution)/shard_map/ppermute | solution.py:19
  11.9 22.2 %collective-permute-start.1 = (bf16[512,576]{0,1:T(8,128)(2,1)}, bf16[512,576]{0,1:T(8,128)(2,1)}, u32[]{:S(2)}, u32[]{:S(2)}) collective-permute-start(bf16[512,576]{0,1:T(8,128)(2,1)} %param.11), channel_id=1, source_target_pairs={{0,16},{8,24},{16,32},{24,40},{32,48},{40,56},{48,64},{56,72},{64,... | collective-permute-start | bytes 1769480 | tf_op jit(solution)/shard_map/ppermute | solution.py:19
  16.5 18.8 %collective-permute-start.2 = (bf16[512,576]{0,1:T(8,128)(2,1)}, bf16[512,576]{0,1:T(8,128)(2,1)S(1)}, u32[]{:S(2)}, u32[]{:S(2)}) collective-permute-start(bf16[512,576]{0,1:T(8,128)(2,1)} %param.11), channel_id=1, source_target_pairs={{0,8},{8,16},{16,24},{24,32},{32,40},{40,48},{48,56},{56,64},{64,7... | collective-permute-start | bytes 1769480 | tf_op jit(solution)/shard_map/ppermute | solution.py:19
  21.3 14.1 %copy-start.2 = (bf16[512,576]{0,1:T(8,128)(2,1)S(1)}, bf16[512,576]{0,1:T(8,128)(2,1)}, u32[]{:S(2)}) copy-start(bf16[512,576]{0,1:T(8,128)(2,1)} %param.11) | copy-start | bytes 1769476
  36.8 1.7 copy-start.3
  121.8 6.8 %collective-permute-start.3 = (f32[512,576]{0,1:T(8,128)S(1)}, f32[512,576]{0,1:T(8,128)S(1)}, u32[]{:S(2)}, u32[]{:S(2)}) collective-permute-start(f32[512,576]{0,1:T(8,128)S(1)} %get-tuple-element.637), channel_id=1, source_target_pairs={{8,0},{16,8},{24,16},{32,24},{40,32},{48,40},{56,48},{64,56},{72,6... | collective-permute-start | bytes 3538952 | tf_op jit(solution)/shard_map/ppermute | solution.py:19
  123.1 39.5 %collective-permute-start.5 = (f32[512,576]{0,1:T(8,128)S(1)}, f32[512,576]{0,1:T(8,128)S(1)}, u32[]{:S(2)}, u32[]{:S(2)}) collective-permute-start(f32[512,576]{0,1:T(8,128)S(1)} %get-tuple-element.638), channel_id=1, source_target_pairs={{24,0},{32,8},{40,16},{48,24},{56,32},{64,40},{72,48},{80,56},{88,... | collective-permute-start | bytes 3538952 | tf_op jit(solution)/shard_map/ppermute | solution.py:19
  124.4 50.3 %collective-permute-start.4 = (f32[512,576]{0,1:T(8,128)S(1)}, f32[512,576]{0,1:T(8,128)S(1)}, u32[]{:S(2)}, u32[]{:S(2)}) collective-permute-start(f32[512,576]{0,1:T(8,128)S(1)} %get-tuple-element.639), channel_id=1, source_target_pairs={{16,0},{24,8},{32,16},{40,24},{48,32},{56,40},{64,48},{72,56},{80,... | collective-permute-start | bytes 3538952 | tf_op jit(solution)/shard_map/ppermute | solution.py:19
  178.1 197.8 %reduce-scatter.4.cloned.1.call-start = ((), (), s32[]{:S(2)}) async-start(), calls=%async_computation.2 | async-start | bytes 1081344
Sparse Core Ops, SparseCore 0:
  178.2 149.2 all-gather.2
Sparse Core Ops, SparseCore 1:
  181.6 194.2 reduce-scatter.3
